TPU v7x, 512 devices: a whole 4x4x16 slice. The times are simulated.
512 devices in a mesh: half: 2 (over core), row: 16 (over z), col: 16 (over y, x).
Axes of the slice: x: 4, y: 4, z: 16, core: 2. Of those that a mesh axis runs over, the one named last changes fastest.
Arguments:
- child_front: float32 [2, 8192, 8192], P('half', 'row', 'col'), as said below
- child_map: int32 [2, 48], P('half'), may hold values from 0 to 63, as said below
- root_front: float32 [8192, 16, 2, 256], P('row', 'col', 'half'), as said below
Outputs:
- child_panel: float32 [2, 512, 8192], P('half', None, 'col')
- root_panel: float32 [512, 16, 2, 256], P(None, 'col', 'half')
- root_update: float32 [8192, 16, 2, 256], P('row', 'col', 'half')
Inputs may be any that keep to these rules, and one draw needn't show every extreme that they name: `child_map`: for child h, the update blocks of row part k (the 3 blocks after that part's first block) map in increasing order to distinct blocks among the root's blocks k * 4 to (k + 1) * 4 - 1. `child_front`: each child's front is symmetric and positive definite. `root_front`: the root front is symmetric and positive definite.
All inputs are finite; a program needn't handle non-finite values.
Results may differ from a plain program's by a relative error of at most 0.0001.
Values sent between devices are 32-bit elements; how exact they have to be, the bound alone decides.
A program may use at most 64 MiB of HBM per device.

v0:
```python
import jax
import jax.numpy as jnp
from jax import lax
from jax.sharding import PartitionSpec as P

BLK = 128
PB = 32


def spread_2(value, axis, source):
    kept = jnp.where(lax.axis_index(axis) == source, value, 0).astype(value.dtype)
    return lax.psum(kept, axis)


def lower_solve(factor, right):
    return lax.linalg.triangular_solve(factor, right, left_side=True, lower=True)


def transposed_product(left, right):
    return lax.dot_general(
        left,
        right,
        (((0,), (0,)), ((), ())),
        precision=lax.Precision.HIGHEST,
        preferred_element_type=jnp.float32,
    )


def selector(child_row_map, part_index, child_tiles, root_tiles):
    per_part = child_tiles - 1
    targets = (
        lax.dynamic_slice_in_dim(child_row_map, part_index * per_part, per_part)
        - part_index * root_tiles
    )
    one_hot = (jnp.arange(root_tiles, dtype=jnp.int32)[:, None] == targets[None, :]).astype(
        jnp.float32
    )
    return jnp.concatenate([jnp.zeros((root_tiles, 1), jnp.float32), one_hot], axis=1)


def body(child_front, child_map, root_front):
    tile_rows = BLK
    pivot_count = PB
    child_block = child_front[0]
    part_rows = child_block.shape[0]
    row_part = lax.axis_index("row")
    col_part = lax.axis_index("col")
    strips = lax.all_gather(child_block[:pivot_count, :], "row", axis=0, tiled=True)
    pieces = lax.all_gather(
        child_block[None, :pivot_count, :pivot_count], ("row", "col"), axis=0, tiled=True
    )
    parts_count = lax.axis_size("row")
    corner = pieces.reshape(parts_count, parts_count, pivot_count, pivot_count).transpose(
        0, 2, 1, 3
    )
    corner = corner.reshape(parts_count * pivot_count, parts_count * pivot_count)
    factor = jnp.linalg.cholesky(corner)
    child_panel = lower_solve(factor, strips)
    columns = lax.all_gather(child_block[:, :pivot_count], "col", axis=1, tiled=True)
    panel_rows = lower_solve(factor, columns.T)
    update = child_block - transposed_product(panel_rows, child_panel)
    root_rows = root_front.shape[0]
    child_tiles = part_rows // tile_rows
    root_tiles = root_rows // tile_rows
    own_map = child_map[0]
    row_select = selector(own_map, row_part, child_tiles, root_tiles)
    col_select = selector(own_map, col_part, child_tiles, root_tiles)
    blocks = update.reshape(child_tiles, tile_rows, child_tiles, tile_rows)
    spread = jnp.einsum("ap,piqj->aiqj", row_select, blocks, precision=lax.Precision.HIGHEST)
    spread = jnp.einsum("aiqj,bq->aibj", spread, col_select, precision=lax.Precision.HIGHEST)
    additions = spread.reshape(root_rows, 2, root_rows // 2)
    joined = lax.psum_scatter(additions, "half", scatter_dimension=1, tiled=True)
    assembled = root_front[:, 0, 0, :] + joined[:, 0, :]
    root_strips = lax.all_gather(assembled[:pivot_count, :], "row", axis=0, tiled=True)
    pivots = spread_2(root_strips[:, :pivot_count], "half", 0)
    root_corner = lax.all_gather(pivots, "col", axis=1, tiled=True)
    root_factor = jnp.linalg.cholesky(root_corner)
    root_panel = lower_solve(root_factor, root_strips)
    mirrored = spread_2(root_panel, "col", row_part)
    both_halves = lax.all_gather(mirrored[:, None, :], "half", axis=1, tiled=True)
    panel_side = both_halves.reshape(both_halves.shape[0], root_rows)
    root_update = assembled - transposed_product(panel_side, root_panel)
    return (child_panel[None], root_panel[:, None, None, :], root_update[:, None, None, :])


def solution(mesh):
    return jax.shard_map(
        body,
        mesh=mesh,
        in_specs=(P("half", "row", "col"), P("half", None), P("row", "col", "half", None)),
        out_specs=(
            P("half", None, "col"),
            P(None, "col", "half", None),
            P("row", "col", "half", None),
        ),
        check_vma=False,
    )
```

profile of v0, /device:TPU:1, one launch (start us, length us, event | category | flops | bytes accessed | tf_op | source)
XLA Modules:
  0.0 844.2 jit_solution(4435899986150828886)
XLA Ops:
  12.8 208.7 %all-gather.14.cloned.1.call-done = f32[8192,32]{1,0:T(8,128)} async-done(((f32[32,32]{1,0:T(8,128)}), f32[8192,32]{1,0:T(8,128)}) %all-gather.14.cloned.1.call-update) | async-done | bytes 1048592 | tf_op jit(solution)/shard_map/all_gather | solution.py:49
  232.2 11.7 %cholesky.286 = f32[128,128]{1,0:T(8,128)S(1)} custom-call(f32[128,128]{1,0:T(8,128)S(1)} %cholesky.426), custom_call_target="Cholesky" | custom-call | tf_op jit(solution)/shard_map/jit(cholesky)/cholesky | solution.py:57
  244.0 9.8 %custom-call.31 = f32[1,128,128]{1,2,0:T(8,128)S(1)} custom-call(f32[1,128,128]{2,1,0:T(8,128)S(1)} %get-tuple-element.79), custom_call_target="InvertDiagBlocksLowerTriangular" | custom-call | tf_op jit(solution)/shard_map/jit(cholesky)/cholesky | solution.py:57
  256.4 11.7 %cholesky.305 = f32[128,128]{1,0:T(8,128)S(1)} custom-call(f32[128,128]{1,0:T(8,128)S(1)} %cholesky.430), custom_call_target="Cholesky" | custom-call | tf_op jit(solution)/shard_map/jit(cholesky)/cholesky | solution.py:57
  268.2 10.0 %custom-call.32 = f32[1,128,128]{1,2,0:T(8,128)S(1)} custom-call(f32[1,128,128]{2,1,0:T(8,128)S(1)} %get-tuple-element.76), custom_call_target="InvertDiagBlocksLowerTriangular" | custom-call | tf_op jit(solution)/shard_map/jit(cholesky)/cholesky | solution.py:57
  279.7 11.7 %cholesky.326 = f32[128,128]{1,0:T(8,128)S(1)} custom-call(f32[128,128]{1,0:T(8,128)S(1)} %cholesky.435), custom_call_target="Cholesky" | custom-call | tf_op jit(solution)/shard_map/jit(cholesky)/cholesky | solution.py:57
  292.2 9.8 %custom-call.33 = f32[1,128,128]{1,2,0:T(8,128)S(1)} custom-call(f32[1,128,128]{2,1,0:T(8,128)S(1)} %get-tuple-element.73), custom_call_target="InvertDiagBlocksLowerTriangular" | custom-call | tf_op jit(solution)/shard_map/jit(cholesky)/cholesky | solution.py:57
  303.5 11.7 %cholesky.343 = f32[128,128]{1,0:T(8,128)S(1)} custom-call(f32[128,128]{1,0:T(8,128)S(1)} %convolution_subtract_fusion.16), custom_call_target="Cholesky" | custom-call | tf_op jit(solution)/shard_map/jit(cholesky)/cholesky | solution.py:57
  319.6 8.5 %while.6 = (s32[]{:T(128)}, f32[512,512]{1,0:T(8,128)S(1)}, s32[4,2]{0,1:T(2,128)S(1)}, f32[4,128,128]{2,1,0:T(8,128)S(1)}, s32[]{:T(128)}) while((s32[]{:T(128)}, f32[512,512]{1,0:T(8,128)S(1)}, s32[4,2]{0,1:T(2,128)S(1)}, f32[4,128,128]{2,1,0:T(8,128)S(1)}, s32[]{:T(128)}) %tuple.64), condition=%wide.while_cond, body=%wide.while_body.sunk | while | flops 2 | bytes 131181 | solution.py:16
  328.1 39.3 %custom-call.34 = f32[4,128,128]{1,2,0:T(8,128)S(1)} custom-call(f32[4,128,128]{2,1,0:T(8,128)S(1)} %get-tuple-element.27), custom_call_target="InvertDiagBlocksLowerTriangular" | custom-call | tf_op jit(solution)/shard_map/triangular_solve/custom-call.3 | solution.py:16
  392.0 23.3 %reduce-scatter.2.cloned.1.call-done = f32[512,1,256]{2,0,1:T(8,128)} async-done(((f32[512,2,256]{2,0,1:T(8,128)}), f32[512,1,256]{2,0,1:T(8,128)}) %reduce-scatter.2.cloned.1.call-update) | async-done | bytes 524304 | tf_op jit(solution)/shard_map/reduce_scatter | solution.py:72
  417.2 25.4 %all_gather.21 = f32[512,256]{1,0:T(8,128)S(1)} all-gather(f32[32,256]{1,0:T(8,128)S(1)} %slice.211), channel_id=1, replica_groups=mesh['half'=2,'row'=16,'col'=16] {'row'}, dimensions={0}, use_global_device_ids=true | all-gather | bytes 557056 | tf_op jit(solution)/shard_map/all_gather | solution.py:74
  443.4 44.3 %all-reduce.6.cloned.1.call-done = f32[512,32]{0,1:T(8,128)} async-done(((f32[512,32]{0,1:T(8,128)}), f32[512,32]{0,1:T(8,128)}) %all-reduce.6.cloned.1.call-update) | async-done | bytes 65552 | tf_op jit(solution)/shard_map/psum | solution.py:12
  487.9 59.6 %all-gather.10.cloned.1.call-done = f32[512,512]{0,1:T(8,128)} async-done(((f32[512,32]{0,1:T(8,128)}), f32[512,512]{0,1:T(8,128)}) %all-gather.10.cloned.1.call-update) | async-done | bytes 1048592 | tf_op jit(solution)/shard_map/all_gather | solution.py:76
  550.5 11.7 %cholesky.358 = f32[128,128]{1,0:T(8,128)S(1)} custom-call(f32[128,128]{1,0:T(8,128)S(1)} %cholesky.439), custom_call_target="Cholesky" | custom-call | tf_op jit(solution)/shard_map/jit(cholesky)/cholesky | solution.py:77
  562.4 9.8 %custom-call.36 = f32[1,128,128]{1,2,0:T(8,128)S(1)} custom-call(f32[1,128,128]{2,1,0:T(8,128)S(1)} %get-tuple-element.69), custom_call_target="InvertDiagBlocksLowerTriangular" | custom-call | tf_op jit(solution)/shard_map/jit(cholesky)/cholesky | solution.py:77
  573.6 11.7 %cholesky.377 = f32[128,128]{1,0:T(8,128)S(1)} custom-call(f32[128,128]{1,0:T(8,128)S(1)} %cholesky.443), custom_call_target="Cholesky" | custom-call | tf_op jit(solution)/shard_map/jit(cholesky)/cholesky | solution.py:77
  586.7 10.0 %custom-call.37 = f32[1,128,128]{1,2,0:T(8,128)S(1)} custom-call(f32[1,128,128]{2,1,0:T(8,128)S(1)} %get-tuple-element.66), custom_call_target="InvertDiagBlocksLowerTriangular" | custom-call | tf_op jit(solution)/shard_map/jit(cholesky)/cholesky | solution.py:77
  598.8 13.2 %cholesky.398 = f32[128,128]{1,0:T(8,128)} custom-call(f32[128,128]{1,0:T(8,128)} %cholesky.448), custom_call_target="Cholesky" | custom-call | tf_op jit(solution)/shard_map/jit(cholesky)/cholesky | solution.py:77
  614.2 11.3 %custom-call.38 = f32[1,128,128]{1,2,0:T(8,128)} custom-call(f32[1,128,128]{2,1,0:T(8,128)} %get-tuple-element.63), custom_call_target="InvertDiagBlocksLowerTriangular" | custom-call | tf_op jit(solution)/shard_map/jit(cholesky)/cholesky | solution.py:77
  626.9 11.7 %cholesky.415 = f32[128,128]{1,0:T(8,128)S(1)} custom-call(f32[128,128]{1,0:T(8,128)S(1)} %convolution_subtract_fusion.15), custom_call_target="Cholesky" | custom-call | tf_op jit(solution)/shard_map/jit(cholesky)/cholesky | solution.py:77
  650.2 39.3 %custom-call.26 = f32[4,128,128]{1,2,0:T(8,128)S(1)} custom-call(f32[4,128,128]{2,1,0:T(8,128)S(1)} %get-tuple-element.20), custom_call_target="InvertDiagBlocksLowerTriangular" | custom-call | tf_op jit(solution)/shard_map/triangular_solve | solution.py:16
  693.7 115.5 %all-reduce.8.cloned.1.call-done = f32[512,1,256]{2,0,1:T(8,128)} async-done(((f32[512,1,256]{2,0,1:T(8,128)}), f32[512,1,256]{2,0,1:T(8,128)}) %all-reduce.8.cloned.1.call-update) | async-done | bytes 524304 | tf_op jit(solution)/shard_map/psum | solution.py:12
  812.5 20.5 %all-gather.12.cloned.1.call-done = f32[512,2,256]{2,0,1:T(8,128)} async-done(((f32[512,1,256]{2,0,1:T(8,128)}), f32[512,2,256]{2,0,1:T(8,128)}) %all-gather.12.cloned.1.call-update) | async-done | bytes 1048592 | tf_op jit(solution)/shard_map/all_gather | solution.py:80
  (154 shorter events, 100.0 us)
Async XLA Ops:
  7.2 214.4 %all-gather.14.cloned.1.call-start = ((), (), s32[]{:S(2)}) async-start(), calls=%async_computation.7 | async-start | bytes 4210688 | tf_op jit(solution)/shard_map/all_gather | solution.py:49
  8.6 358.9 %all-gather.8.cloned.1.call-start = ((), (), s32[]{:S(2)}) async-start(), calls=%async_computation.1 | async-start | bytes 1114112 | tf_op jit(solution)/shard_map/all_gather | solution.py:59
  10.3 365.5 %all-gather.16.cloned.1.call-start = ((), (), s32[]{:S(2)}) async-start(), calls=%async_computation.8 | async-start | bytes 1114112 | tf_op jit(solution)/shard_map/all_gather | solution.py:48
  11.9 403.3 %reduce-scatter.2.cloned.1.call-start = ((), (), s32[]{:S(2)}) async-start(), calls=%async_computation.2 | async-start | bytes 1572864 | tf_op jit(solution)/shard_map/reduce_scatter | solution.py:72
  231.2 1.0 copy-start
  372.4 0.7 copy-start.3
  375.8 7.7 copy-start.4
  375.8 7.7 copy-start.9
  382.9 0.7 copy-start.5
  388.7 26.5 %copy-start.7 = (f32[512,1,1,256]{3,2,1,0:T(1,128)S(1)}, f32[512,1,1,256]{3,2,1,0:T(1,128)}, u32[]{:S(2)}) copy-start(f32[512,1,1,256]{3,2,1,0:T(1,128)} %param.8) | copy-start | bytes 1572868
  391.9 95.8 %all-reduce.6.cloned.1.call-start = ((), (), s32[]{:S(2)}) async-start(), calls=%async_computation.3 | async-start | bytes 131072 | tf_op jit(solution)/shard_map/psum | solution.py:12
  416.4 0.8 copy-start.1
  443.3 104.2 %all-gather.10.cloned.1.call-start = ((), (), s32[]{:S(2)}) async-start(), calls=%async_computation.4 | async-start | bytes 1114112 | tf_op jit(solution)/shard_map/all_gather | solution.py:76
  487.7 321.4 %all-reduce.8.cloned.1.call-start = ((), (), s32[]{:S(2)}) async-start(), calls=%async_computation.5 | async-start | bytes 1048576 | tf_op jit(solution)/shard_map/psum | solution.py:12
  572.9 0.7 copy-start.6
  689.6 1.5 copy-start.8
  691.5 143.1 %copy-start.2 = (f32[512,256]{1,0:T(8,128)S(1)}, f32[512,256]{1,0:T(8,128)}, u32[]{:S(2)}) copy-start(f32[512,256]{1,0:T(8,128)} %copy-done.1) | copy-start | bytes 1572868
  693.6 139.4 %all-gather.12.cloned.1.call-start = ((), (), s32[]{:S(2)}) async-start(), calls=%async_computation.6 | async-start | bytes 1572864 | tf_op jit(solution)/shard_map/all_gather | solution.py:80
Sparse Core Ops, SparseCore 0:
  13.1 208.4 all-gather.13
  225.1 59.4 all-gather.7
  287.2 63.2 all-gather.15
  392.0 23.1 reduce-scatter.1
  443.5 44.1 all-reduce.5
  491.0 56.4 all-gather.9
  693.7 115.3 all-reduce.7
  811.2 21.7 all-gather.11
where the time goes:
time: 855 us; the launch traced here: 844 us
  waiting for transfers between devices  472 us (55%)
  other arithmetic  248 us (29%)
  local copies, waits for them, and re-layouts  43.7 us (5%)
  matrix products  33.6 us (4%)
  blocking collectives  25.4 us (3%)
  between operations  20.3 us (2%)
    all_gather x1, waiting for transfers between devices, body(): lax.all_gather(child_block[None, :pivot_count, :pivot_count], ('row', 'co...  209 us
    psum x2, waiting for transfers between devices, spread_2(): return lax.psum(kept, axis)  160 us
    another operation x15, other arithmetic, body(): root_factor = jnp.linalg.cholesky(root_corner)  83.6 us
    another operation x5, other arithmetic, lower_solve(): lax.linalg.triangular_solve(factor, right, left_side=True, lower=True)  79.1 us
    another operation x14, other arithmetic, body(): factor = jnp.linalg.cholesky(corner)  78.6 us
    all_gather x1, waiting for transfers between devices, body(): root_corner = lax.all_gather(pivots, 'col', axis=1, tiled=True)  59.6 us
    all_gather x1, blocking collectives, body(): lax.all_gather(assembled[:pivot_count, :], 'row', axis=0, tiled=True)  25.4 us
    reduce_scatter x1, waiting for transfers between devices, body(): lax.psum_scatter(additions, 'half', scatter_dimension=1, tiled=True)  23.3 us
  transfers between devices with their start and end apart: 8, of which 6 were waited for; matrix products, arithmetic and copies ran while one was open for 19% of the time, Pallas kernels for 0%

commit v1 on v0

--- a/solution.py
+++ b/solution.py
@@ -1,3 +1,4 @@
+import functools
 import jax
 import jax.numpy as jnp
 from jax import lax
@@ -5,6 +6,18 @@
 
 BLK = 128
 PB = 32
+
+
+def answer_plate(base_x, which_dim):
+    by_place = []
+    for _ in range(lax.axis_size("col")):
+        by_place.append(base_x)
+    w1 = lax.all_to_all(jnp.stack(by_place), axis_name="col", split_axis=0, concat_axis=0)
+    a_now = jnp.concatenate(w1, axis=which_dim)
+    return a_now
+
+
+members_all_load = functools.partial(answer_plate, which_dim=1)
 
 
 def spread_2(value, axis, source):
@@ -73,7 +86,7 @@
     assembled = root_front[:, 0, 0, :] + joined[:, 0, :]
     root_strips = lax.all_gather(assembled[:pivot_count, :], "row", axis=0, tiled=True)
     pivots = spread_2(root_strips[:, :pivot_count], "half", 0)
-    root_corner = lax.all_gather(pivots, "col", axis=1, tiled=True)
+    root_corner = members_all_load(pivots)
     root_factor = jnp.linalg.cholesky(root_corner)
     root_panel = lower_solve(root_factor, root_strips)
     mirrored = spread_2(root_panel, "col", row_part)

time: 855 us -> 813 us (0.951)
  waiting for transfers between devices: 472 us -> 428 us
    all_gather x1 -> x0, waiting for transfers between devices: 59.6 us -> none  [body(): root_corner = lax.all_gather(pivots, 'col', axis=1, tiled=True)]
    all_to_all x0 -> x1, waiting for transfers between devices: none -> 16.3 us  [answer_plate(): lax.all_to_all(jnp.stack(by_place), axis_name='col', split_axis=0, concat...]
  transfers between devices with their start and end apart: 8 -> 8, of which waited for: 6 -> 6; matrix products, arithmetic and copies ran while one was open for 19% -> 20% of each run, Pallas kernels for 0% -> 0%
where the time goes in v1:
time: 813 us; the launch traced here: 802 us
  waiting for transfers between devices  428 us (53%)
  other arithmetic  243 us (30%)
  local copies, waits for them, and re-layouts  43.8 us (5%)
  matrix products  35.5 us (4%)
  blocking collectives  25.4 us (3%)
  between operations  20.3 us (2%)
    all_gather x1, waiting for transfers between devices, body(): lax.all_gather(child_block[None, :pivot_count, :pivot_count], ('row', 'co...  209 us
    psum x2, waiting for transfers between devices, spread_2(): return lax.psum(kept, axis)  159 us
    another operation x5, other arithmetic, lower_solve(): lax.linalg.triangular_solve(factor, right, left_side=True, lower=True)  79.5 us
    another operation x15, other arithmetic, body(): root_factor = jnp.linalg.cholesky(root_corner)  79.2 us
    another operation x14, other arithmetic, body(): factor = jnp.linalg.cholesky(corner)  78.6 us
    all_gather x1, blocking collectives, body(): lax.all_gather(assembled[:pivot_count, :], 'row', axis=0, tiled=True)  25.4 us
    reduce_scatter x1, waiting for transfers between devices, body(): lax.psum_scatter(additions, 'half', scatter_dimension=1, tiled=True)  23.3 us
    all_gather x1, waiting for transfers between devices, body(): lax.all_gather(mirrored[:, None, :], 'half', axis=1, tiled=True)  20.7 us
  transfers between devices with their start and end apart: 8, of which 6 were waited for; matrix products, arithmetic and copies ran while one was open for 20% of the time, Pallas kernels for 0%

profile of v1, /device:TPU:1, one launch (start us, length us, event | category | flops | bytes accessed | tf_op | source)
XLA Modules:
  0.0 802.4 jit_solution(15668333136225276405)
XLA Ops:
  12.8 208.7 %all-gather.11.cloned.1.call-done = f32[8192,32]{1,0:T(8,128)} async-done(((f32[32,32]{1,0:T(8,128)}), f32[8192,32]{1,0:T(8,128)}) %all-gather.11.cloned.1.call-update) | async-done | bytes 1048592 | tf_op jit(solution)/shard_map/all_gather | solution.py:62
  232.2 11.7 %cholesky.286 = f32[128,128]{1,0:T(8,128)S(1)} custom-call(f32[128,128]{1,0:T(8,128)S(1)} %cholesky.426), custom_call_target="Cholesky" | custom-call | tf_op jit(solution)/shard_map/jit(cholesky)/cholesky | solution.py:70
  244.0 9.8 %custom-call.31 = f32[1,128,128]{1,2,0:T(8,128)S(1)} custom-call(f32[1,128,128]{2,1,0:T(8,128)S(1)} %get-tuple-element.79), custom_call_target="InvertDiagBlocksLowerTriangular" | custom-call | tf_op jit(solution)/shard_map/jit(cholesky)/cholesky | solution.py:70
  256.4 11.7 %cholesky.305 = f32[128,128]{1,0:T(8,128)S(1)} custom-call(f32[128,128]{1,0:T(8,128)S(1)} %cholesky.430), custom_call_target="Cholesky" | custom-call | tf_op jit(solution)/shard_map/jit(cholesky)/cholesky | solution.py:70
  268.2 10.0 %custom-call.32 = f32[1,128,128]{1,2,0:T(8,128)S(1)} custom-call(f32[1,128,128]{2,1,0:T(8,128)S(1)} %get-tuple-element.76), custom_call_target="InvertDiagBlocksLowerTriangular" | custom-call | tf_op jit(solution)/shard_map/jit(cholesky)/cholesky | solution.py:70
  279.7 11.7 %cholesky.326 = f32[128,128]{1,0:T(8,128)S(1)} custom-call(f32[128,128]{1,0:T(8,128)S(1)} %cholesky.435), custom_call_target="Cholesky" | custom-call | tf_op jit(solution)/shard_map/jit(cholesky)/cholesky | solution.py:70
  292.2 9.8 %custom-call.33 = f32[1,128,128]{1,2,0:T(8,128)S(1)} custom-call(f32[1,128,128]{2,1,0:T(8,128)S(1)} %get-tuple-element.73), custom_call_target="InvertDiagBlocksLowerTriangular" | custom-call | tf_op jit(solution)/shard_map/jit(cholesky)/cholesky | solution.py:70
  303.5 11.7 %cholesky.343 = f32[128,128]{1,0:T(8,128)S(1)} custom-call(f32[128,128]{1,0:T(8,128)S(1)} %convolution_subtract_fusion.16), custom_call_target="Cholesky" | custom-call | tf_op jit(solution)/shard_map/jit(cholesky)/cholesky | solution.py:70
  319.2 8.5 %while.6 = (s32[]{:T(128)}, f32[512,512]{1,0:T(8,128)S(1)}, s32[4,2]{0,1:T(2,128)S(1)}, f32[4,128,128]{2,1,0:T(8,128)S(1)}, s32[]{:T(128)}) while((s32[]{:T(128)}, f32[512,512]{1,0:T(8,128)S(1)}, s32[4,2]{0,1:T(2,128)S(1)}, f32[4,128,128]{2,1,0:T(8,128)S(1)}, s32[]{:T(128)}) %tuple.64), condition=%wide.while_cond, body=%wide.while_body.sunk | while | flops 2 | bytes 131181 | solution.py:29
  327.7 39.7 %custom-call.34 = f32[4,128,128]{1,2,0:T(8,128)S(1)} custom-call(f32[4,128,128]{2,1,0:T(8,128)S(1)} %get-tuple-element.27), custom_call_target="InvertDiagBlocksLowerTriangular" | custom-call | tf_op jit(solution)/shard_map/triangular_solve/custom-call.3 | solution.py:29
  392.0 23.3 %reduce-scatter.2.cloned.1.call-done = f32[512,1,256]{2,0,1:T(8,128)} async-done(((f32[512,2,256]{2,0,1:T(8,128)}), f32[512,1,256]{2,0,1:T(8,128)}) %reduce-scatter.2.cloned.1.call-update) | async-done | bytes 524304 | tf_op jit(solution)/shard_map/reduce_scatter | solution.py:85
  417.2 25.4 %all_gather.18 = f32[512,256]{1,0:T(8,128)S(1)} all-gather(f32[32,256]{1,0:T(8,128)S(1)} %slice.211), channel_id=1, replica_groups=mesh['half'=2,'row'=16,'col'=16] {'row'}, dimensions={0}, use_global_device_ids=true | all-gather | bytes 557056 | tf_op jit(solution)/shard_map/all_gather | solution.py:87
  443.3 44.9 %all-reduce.6.cloned.1.call-done = f32[512,32]{1,0:T(8,128)} async-done(((f32[512,32]{1,0:T(8,128)}), f32[512,32]{1,0:T(8,128)}) %all-reduce.6.cloned.1.call-update) | async-done | bytes 65552 | tf_op jit(solution)/shard_map/psum | solution.py:25
  496.1 16.3 %all-to-all-done = f32[16,512,32]{1,2,0:T(8,128)S(1)} async-done(((f32[16,512,32]{1,2,0:T(8,128)}), f32[16,512,32]{1,2,0:T(8,128)S(1)}, u32[]{:S(2)}, u32[]{:S(2)}) %all-to-all-start) | async-done | bytes 1048608 | tf_op jit(solution)/shard_map/all_to_all | solution.py:15
  514.0 11.7 %cholesky.358 = f32[128,128]{1,0:T(8,128)S(1)} custom-call(f32[128,128]{1,0:T(8,128)S(1)} %cholesky.439), custom_call_target="Cholesky" | custom-call | tf_op jit(solution)/shard_map/jit(cholesky)/cholesky | solution.py:90
  525.9 9.8 %custom-call.36 = f32[1,128,128]{1,2,0:T(8,128)S(1)} custom-call(f32[1,128,128]{2,1,0:T(8,128)S(1)} %get-tuple-element.69), custom_call_target="InvertDiagBlocksLowerTriangular" | custom-call | tf_op jit(solution)/shard_map/jit(cholesky)/cholesky | solution.py:90
  538.2 11.7 %cholesky.377 = f32[128,128]{1,0:T(8,128)S(1)} custom-call(f32[128,128]{1,0:T(8,128)S(1)} %cholesky.443), custom_call_target="Cholesky" | custom-call | tf_op jit(solution)/shard_map/jit(cholesky)/cholesky | solution.py:90
  551.3 10.0 %custom-call.37 = f32[1,128,128]{1,2,0:T(8,128)S(1)} custom-call(f32[1,128,128]{2,1,0:T(8,128)S(1)} %get-tuple-element.66), custom_call_target="InvertDiagBlocksLowerTriangular" | custom-call | tf_op jit(solution)/shard_map/jit(cholesky)/cholesky | solution.py:90
  562.9 11.7 %cholesky.398 = f32[128,128]{1,0:T(8,128)S(1)} custom-call(f32[128,128]{1,0:T(8,128)S(1)} %cholesky.448), custom_call_target="Cholesky" | custom-call | tf_op jit(solution)/shard_map/jit(cholesky)/cholesky | solution.py:90
  575.3 9.8 %custom-call.38 = f32[1,128,128]{1,2,0:T(8,128)S(1)} custom-call(f32[1,128,128]{2,1,0:T(8,128)S(1)} %get-tuple-element.63), custom_call_target="InvertDiagBlocksLowerTriangular" | custom-call | tf_op jit(solution)/shard_map/jit(cholesky)/cholesky | solution.py:90
  586.5 11.7 %cholesky.415 = f32[128,128]{1,0:T(8,128)S(1)} custom-call(f32[128,128]{1,0:T(8,128)S(1)} %convolution_subtract_fusion.15), custom_call_target="Cholesky" | custom-call | tf_op jit(solution)/shard_map/jit(cholesky)/cholesky | solution.py:90
  609.9 39.3 %custom-call.26 = f32[4,128,128]{1,2,0:T(8,128)S(1)} custom-call(f32[4,128,128]{2,1,0:T(8,128)S(1)} %get-tuple-element.20), custom_call_target="InvertDiagBlocksLowerTriangular" | custom-call | tf_op jit(solution)/shard_map/triangular_solve | solution.py:29
  653.3 113.8 %all-reduce.8.cloned.1.call-done = f32[512,1,256]{2,0,1:T(8,128)} async-done(((f32[512,1,256]{2,0,1:T(8,128)}), f32[512,1,256]{2,0,1:T(8,128)}) %all-reduce.8.cloned.1.call-update) | async-done | bytes 524304 | tf_op jit(solution)/shard_map/psum | solution.py:25
  770.5 20.7 %all-gather.9.cloned.1.call-done = f32[512,2,256]{2,0,1:T(8,128)} async-done(((f32[512,1,256]{2,0,1:T(8,128)}), f32[512,2,256]{2,0,1:T(8,128)}) %all-gather.9.cloned.1.call-update) | async-done | bytes 1048592 | tf_op jit(solution)/shard_map/all_gather | solution.py:93
  (153 shorter events, 104.9 us)
Async XLA Ops:
  7.2 214.4 %all-gather.11.cloned.1.call-start = ((), (), s32[]{:S(2)}) async-start(), calls=%async_computation.7 | async-start | bytes 4210688 | tf_op jit(solution)/shard_map/all_gather | solution.py:62
  8.6 358.9 %all-gather.7.cloned.1.call-start = ((), (), s32[]{:S(2)}) async-start(), calls=%async_computation.2 | async-start | bytes 1114112 | tf_op jit(solution)/shard_map/all_gather | solution.py:72
  10.3 365.5 %all-gather.13.cloned.1.call-start = ((), (), s32[]{:S(2)}) async-start(), calls=%async_computation.8 | async-start | bytes 1114112 | tf_op jit(solution)/shard_map/all_gather | solution.py:61
  11.9 403.3 %reduce-scatter.2.cloned.1.call-start = ((), (), s32[]{:S(2)}) async-start(), calls=%async_computation.3 | async-start | bytes 1572864 | tf_op jit(solution)/shard_map/reduce_scatter | solution.py:85
  231.2 1.0 copy-start.1
  372.4 0.7 copy-start.4
  375.8 7.7 copy-start.5
  375.8 7.7 copy-start.9
  382.9 0.7 copy-start.6
  388.7 26.5 %copy-start.7 = (f32[512,1,1,256]{3,2,1,0:T(1,128)S(1)}, f32[512,1,1,256]{3,2,1,0:T(1,128)}, u32[]{:S(2)}) copy-start(f32[512,1,1,256]{3,2,1,0:T(1,128)} %param.8) | copy-start | bytes 1572868
  391.9 96.3 %all-reduce.6.cloned.1.call-start = ((), (), s32[]{:S(2)}) async-start(), calls=%async_computation.4 | async-start | bytes 524288 | tf_op jit(solution)/shard_map/psum | solution.py:25
  416.4 0.8 copy-start.2
  490.3 22.1 %all-to-all-start = ((f32[16,512,32]{1,2,0:T(8,128)}), f32[16,512,32]{1,2,0:T(8,128)S(1)}, u32[]{:S(2)}, u32[]{:S(2)}) async-start(f32[16,512,32]{1,2,0:T(8,128)} %stack.2), calls=%async_computation.1 | async-start | bytes 2097152 | tf_op jit(solution)/shard_map/all_to_all | solution.py:15
  496.1 271.1 %all-reduce.8.cloned.1.call-start = ((), (), s32[]{:S(2)}) async-start(), calls=%async_computation.5 | async-start | bytes 1048576 | tf_op jit(solution)/shard_map/psum | solution.py:25
  513.0 1.0 copy-start
  649.2 1.5 copy-start.8
  651.1 141.6 %copy-start.3 = (f32[512,256]{1,0:T(8,128)S(1)}, f32[512,256]{1,0:T(8,128)}, u32[]{:S(2)}) copy-start(f32[512,256]{1,0:T(8,128)} %copy-done.2) | copy-start | bytes 1572868
  653.3 137.9 %all-gather.9.cloned.1.call-start = ((), (), s32[]{:S(2)}) async-start(), calls=%async_computation.6 | async-start | bytes 1572864 | tf_op jit(solution)/shard_map/all_gather | solution.py:93
Sparse Core Ops, SparseCore 0:
  13.1 208.4 all-gather.10
  225.1 59.4 all-gather.6
  287.2 63.3 all-gather.12
  392.0 23.1 reduce-scatter.1
  443.4 44.7 all-reduce.5
  653.4 113.7 all-reduce.7
  769.4 21.7 all-gather.8
